TPU v7x, 256 devices: a whole 4x4x8 slice. The times are simulated.
256 devices in a mesh: grid: 16 (over z_hi, y, core), mesh: 16 (over z_lo, x).
Axes of the slice: x: 4, y: 4, z: 8 (z_hi: 2, z_lo: 4; z = z_hi * 4 + z_lo), core: 2. Of those that a mesh axis runs over, the one named last changes fastest.
Arguments:
- grid_latent: bfloat16 [65536, 512], P(('grid', 'mesh')), may hold values from -6 to 6
- mesh_latent: bfloat16 [32768, 512], P(('grid', 'mesh')), may hold values from -6 to 6
- mesh_cotangent: bfloat16 [32768, 512], P(('grid', 'mesh')), may hold values from -6 to 6
- weights: bfloat16 [12, 512, 512], replicated, may hold values from -0.25 to 0.25
- biases: float32 [4, 512], replicated, may hold values from -3 to 3
- norm_gains: float32 [4, 512], replicated, may hold values from 0.25 to 1.75
- grid_send_rows: int32 [256, 16, 16], P(('grid', 'mesh')), may hold values from 0 to 255
- grid_edge_counts: int32 [256, 16], P(('grid', 'mesh')), may hold values from 1 to 16, as said below
- grid_edge_targets: int32 [256, 3, 16, 16], P(('grid', 'mesh')), may hold values from -1 to 127, as said below
- mesh_senders: int32 [256, 512], P(('grid', 'mesh')), may hold values from 0 to 383
- mesh_receivers: int32 [256, 512], P(('grid', 'mesh')), may hold values from 0 to 127
- halo_rows: int32 [256, 16, 16], P(('grid', 'mesh')), may hold values from 0 to 127
Outputs:
- mesh_out: bfloat16 [32768, 512], P(('grid', 'mesh'))
- grid_grad: float32 [65536, 512], P(('grid', 'mesh'))
- mesh_grad: float32 [32768, 512], P(('grid', 'mesh'))
- weight_grad: float32 [4, 787456], P(None, ('grid', 'mesh'))
Inputs may be any that keep to these rules, and one draw needn't show every extreme that they name: `grid_edge_counts`: at most 16 live slots come from one source block to one receiving block, and in every draw some receiving block gets 16 from each of its 16 sources; entries at or past the count carry no edge. `grid_edge_targets`: -1 marks an absent edge; edge position 0 of a slot is never absent.
All inputs are finite; a program needn't handle non-finite values.
Results may differ from a plain program's by a relative error of at most 0.023.
Values may be sent and summed in bfloat16 or wider, within the bound.
A program may use at most 128 MiB of HBM per device.

v0:
```python
import math

import jax
import jax.numpy as jnp
from jax import lax
from jax.sharding import PartitionSpec as P

epsilon = 1e-05


def project(left, weight):
    return jnp.dot(left, weight, preferred_element_type=jnp.float32)


def row_contract(left, right):
    return lax.dot_general(
        left, right, (((0,), (0,)), ((), ())), preferred_element_type=jnp.float32
    )


def through_weight(grad, weight):
    return lax.dot_general(
        grad, weight, (((1,), (1,)), ((), ())), preferred_element_type=jnp.float32
    )


def swish_slope(values):
    sigmoid_value = jax.nn.sigmoid(values)
    return sigmoid_value * (1.0 + values * (1.0 - sigmoid_value))


def perceptron(summed, offset, out_weight, scales):
    hidden = jax.nn.silu(summed + offset).astype(jnp.bfloat16)
    projected = project(hidden, out_weight)
    centered = projected - jnp.mean(projected, axis=-1, keepdims=True)
    reciprocal = lax.rsqrt(jnp.mean(centered * centered, axis=-1, keepdims=True) + epsilon)
    normed = centered * reciprocal
    return (normed * scales, hidden, normed, reciprocal)


def perceptron_back(upstream, summed, offset, out_weight, scales, hidden, normed, reciprocal):
    scale_grad = jnp.sum(upstream * normed, axis=0)
    weighted = upstream * scales
    inner_grad = reciprocal * (
        weighted
        - jnp.mean(weighted, axis=-1, keepdims=True)
        - normed * jnp.mean(weighted * normed, axis=-1, keepdims=True)
    )
    inner_half = inner_grad.astype(jnp.bfloat16)
    matrix_grad = row_contract(hidden, inner_half)
    hidden_grad = through_weight(inner_half, out_weight)
    summed_grad = hidden_grad * swish_slope(summed + offset)
    offset_grad = jnp.sum(summed_grad, axis=0)
    return (summed_grad.astype(jnp.bfloat16), matrix_grad, offset_grad, scale_grad)


def pack_bucket(first, second, third, offset_grad, scale_grad):
    return jnp.concatenate(
        [first.reshape(-1), second.reshape(-1), third.reshape(-1), offset_grad, scale_grad]
    )


def local(
    grid_latent,
    mesh_latent,
    mesh_cotangent,
    weights,
    biases,
    norm_gains,
    grid_send_rows,
    grid_edge_counts,
    grid_edge_targets,
    mesh_senders,
    mesh_receivers,
    halo_rows,
):
    features = grid_latent.shape[1]
    node_count = mesh_latent.shape[0]
    grid_count = grid_latent.shape[0]
    slot_rows = grid_send_rows[0]
    sources, capacity = slot_rows.shape
    targets = grid_edge_targets[0]
    fanout = targets.shape[0]
    halo_list = halo_rows[0]
    peer_count, halo_depth = halo_list.shape
    senders = mesh_senders[0]
    receivers = mesh_receivers[0]
    live_slots = jnp.arange(capacity)[None, :] < grid_edge_counts[0][:, None]
    present = (live_slots[None] & (targets >= 0)).reshape(-1, 1).astype(jnp.float32)
    target_index = jnp.where(targets >= 0, targets, 0).reshape(-1)
    incoming = lax.all_to_all(
        grid_latent[slot_rows], "grid", split_axis=0, concat_axis=0, tiled=True
    )
    slot_terms = project(incoming.reshape(-1, features), weights[0]).astype(jnp.bfloat16)
    grid_summed = (
        jnp.tile(slot_terms.astype(jnp.float32), (fanout, 1))
        + project(mesh_latent, weights[1])[target_index]
    )
    grid_out, grid_hidden, grid_normed, grid_inverse = perceptron(
        grid_summed, biases[0], weights[2], norm_gains[0]
    )
    grid_gathered = jax.ops.segment_sum(
        grid_out * present, target_index, num_segments=node_count
    ).astype(jnp.bfloat16)
    low_summed = project(mesh_latent, weights[3]) + project(grid_gathered, weights[4])
    low_out, low_hidden, low_normed, low_inverse = perceptron(
        low_summed, biases[1], weights[5], norm_gains[1]
    )
    middle = (mesh_latent.astype(jnp.float32) + low_out).astype(jnp.bfloat16)
    halo_terms = lax.all_to_all(middle[halo_list], "mesh", split_axis=0, concat_axis=0, tiled=True)
    joined_rows = jnp.concatenate([middle, halo_terms.reshape(-1, features)], axis=0)
    sender_table = project(joined_rows, weights[6]).astype(jnp.bfloat16)
    mesh_summed = sender_table[senders].astype(jnp.float32) + project(middle, weights[7])[receivers]
    edge_out, mesh_hidden, mesh_normed, mesh_inverse = perceptron(
        mesh_summed, biases[2], weights[8], norm_gains[2]
    )
    mesh_gathered = jax.ops.segment_sum(edge_out, receivers, num_segments=node_count).astype(
        jnp.bfloat16
    )
    top_summed = project(middle, weights[9]) + project(mesh_gathered, weights[10])
    top_out, top_hidden, top_normed, top_inverse = perceptron(
        top_summed, biases[3], weights[11], norm_gains[3]
    )
    mesh_out = (middle.astype(jnp.float32) + top_out).astype(jnp.bfloat16)
    upstream = mesh_cotangent.astype(jnp.float32)
    top_grad, top_weight_grad, top_offset_grad, top_scale_grad = perceptron_back(
        upstream,
        top_summed,
        biases[3],
        weights[11],
        norm_gains[3],
        top_hidden,
        top_normed,
        top_inverse,
    )
    middle_grad = upstream + through_weight(top_grad, weights[9])
    mesh_gathered_grad = through_weight(top_grad, weights[10])
    top_bucket = pack_bucket(
        row_contract(middle, top_grad),
        row_contract(mesh_gathered, top_grad),
        top_weight_grad,
        top_offset_grad,
        top_scale_grad,
    )
    edge_grad, edge_weight_grad, edge_offset_grad, edge_scale_grad = perceptron_back(
        mesh_gathered_grad[receivers],
        mesh_summed,
        biases[2],
        weights[8],
        norm_gains[2],
        mesh_hidden,
        mesh_normed,
        mesh_inverse,
    )
    edge_float = edge_grad.astype(jnp.float32)
    receiver_half = jax.ops.segment_sum(edge_float, receivers, num_segments=node_count).astype(
        jnp.bfloat16
    )
    table_grad = jax.ops.segment_sum(
        edge_float, senders, num_segments=node_count + peer_count * halo_depth
    )
    halo_grad = (
        table_grad[node_count:].reshape(peer_count, halo_depth, features).astype(jnp.bfloat16)
    )
    halo_back = lax.all_to_all(halo_grad, "mesh", split_axis=0, concat_axis=0, tiled=True)
    returned = jax.ops.segment_sum(
        halo_back.reshape(-1, features).astype(jnp.float32),
        halo_list.reshape(-1),
        num_segments=node_count,
    )
    sender_half = (table_grad[:node_count] + returned).astype(jnp.bfloat16)
    middle_grad = (
        middle_grad
        + through_weight(sender_half, weights[6])
        + through_weight(receiver_half, weights[7])
    )
    edge_bucket = pack_bucket(
        row_contract(middle, sender_half),
        row_contract(middle, receiver_half),
        edge_weight_grad,
        edge_offset_grad,
        edge_scale_grad,
    )
    low_grad, low_weight_grad, low_offset_grad, low_scale_grad = perceptron_back(
        middle_grad,
        low_summed,
        biases[1],
        weights[5],
        norm_gains[1],
        low_hidden,
        low_normed,
        low_inverse,
    )
    lower_grad = middle_grad + through_weight(low_grad, weights[3])
    grid_gathered_grad = through_weight(low_grad, weights[4])
    node_bucket = pack_bucket(
        row_contract(mesh_latent, low_grad),
        row_contract(grid_gathered, low_grad),
        low_weight_grad,
        low_offset_grad,
        low_scale_grad,
    )
    grid_edge_grad, grid_weight_grad, grid_offset_grad, grid_scale_grad = perceptron_back(
        grid_gathered_grad[target_index] * present,
        grid_summed,
        biases[0],
        weights[2],
        norm_gains[0],
        grid_hidden,
        grid_normed,
        grid_inverse,
    )
    grid_float = grid_edge_grad.astype(jnp.float32)
    receiver_low = jax.ops.segment_sum(grid_float, target_index, num_segments=node_count).astype(
        jnp.bfloat16
    )
    slot_grad = jnp.sum(grid_float.reshape(fanout, sources, capacity, features), axis=0).astype(
        jnp.bfloat16
    )
    slots_back = lax.all_to_all(slot_grad, "grid", split_axis=0, concat_axis=0, tiled=True)
    grid_half = jax.ops.segment_sum(
        slots_back.reshape(-1, features).astype(jnp.float32),
        slot_rows.reshape(-1),
        num_segments=grid_count,
    ).astype(jnp.bfloat16)
    grid_grad = through_weight(grid_half, weights[0])
    mesh_grad = lower_grad + through_weight(receiver_low, weights[1])
    grid_bucket = pack_bucket(
        row_contract(grid_latent, grid_half),
        row_contract(mesh_latent, receiver_low),
        grid_weight_grad,
        grid_offset_grad,
        grid_scale_grad,
    )
    stacked = jnp.stack([grid_bucket, node_bucket, edge_bucket, top_bucket])
    shares = lax.psum_scatter(stacked, ("grid", "mesh"), scatter_dimension=1, tiled=True)
    grad_scale = 1.0 / math.sqrt(node_count * lax.axis_size("grid") * lax.axis_size("mesh"))
    return (mesh_out, grid_grad, mesh_grad, shares * grad_scale)


def solution(mesh):
    placed = (
        P(("grid", "mesh"), None),
        P(("grid", "mesh"), None),
        P(("grid", "mesh"), None),
        P(),
        P(),
        P(),
        P(("grid", "mesh"), None, None),
        P(("grid", "mesh"), None),
        P(("grid", "mesh"), None, None, None),
        P(("grid", "mesh"), None),
        P(("grid", "mesh"), None),
        P(("grid", "mesh"), None, None),
    )
    return jax.shard_map(
        local,
        mesh=mesh,
        in_specs=placed,
        out_specs=(
            P(("grid", "mesh"), None),
            P(("grid", "mesh"), None),
            P(("grid", "mesh"), None),
            P(None, ("grid", "mesh")),
        ),
        check_vma=False,
    )
```

profile of v0, /device:TPU:6, one launch (start us, length us, event | category | flops | bytes accessed | tf_op | source)
XLA Modules:
  0.0 534.7 jit_solution(14063512884993550788)
XLA Ops:
  10.7 11.2 %all-to-all-start = ((bf16[16,16,512]{2,1,0:T(8,128)(2,1)}), bf16[16,16,512]{2,1,0:T(8,128)(2,1)S(1)}, u32[]{:S(2)}, u32[]{:S(2)}) async-start(bf16[16,16,512]{2,1,0:T(8,128)(2,1)} %bitcast.2), calls=%async_computation | async-start | bytes 524288 | tf_op jit(solution)/shard_map/all_to_all | solution.py:91
  43.2 7.3 %scatter_custom_fusion = f32[128,512]{1,0:T(8,128)S(1)} fusion(s32[768]{0:T(1024)} %get-tuple-element.17, f32[768,512]{1,0:T(8,128)} %copy.27, f32[]{:T(128)} %constant.20.clone.1), kind=kCustom, calls=%fused_computation.173 | custom fusion | flops 393216 | bytes 262656 | tf_op jit(solution)/shard_map/scatter-add | solution.py:102
  56.2 7.0 %all-to-all-start.1 = ((bf16[16,16,512]{2,1,0:T(8,128)(2,1)}), bf16[16,16,512]{2,1,0:T(8,128)(2,1)}, u32[]{:S(2)}, u32[]{:S(2)}) async-start(bf16[16,16,512]{2,1,0:T(8,128)(2,1)} %bitcast.19), calls=%async_computation.1 | async-start | bytes 524288 | tf_op jit(solution)/shard_map/all_to_all | solution.py:110
  66.2 2.4 fusion.29
  68.6 2.8 all-to-all-done.1
  73.0 2.6 gather_fusion.3
  80.7 2.6 copy.28
  83.2 4.5 scatter_custom_fusion.1
  97.5 2.3 convolution_bitcast_fusion.2
  101.2 2.4 gather_fusion.5
  103.7 2.6 copy.29
  106.2 2.3 multiply_reduce_fusion.3
  110.1 3.4 fusion.121
  114.9 4.4 scatter_custom_fusion.4
  119.3 5.2 scatter_custom_fusion.2
  126.3 7.0 %all-to-all-start.2 = ((bf16[16,16,512]{2,1,0:T(8,128)(2,1)}), bf16[16,16,512]{2,1,0:T(8,128)(2,1)}, u32[]{:S(2)}, u32[]{:S(2)}) async-start(bf16[16,16,512]{2,1,0:T(8,128)(2,1)} %bitcast.220), calls=%async_computation.2 | async-start | bytes 524288 | tf_op jit(solution)/shard_map/all_to_all | solution.py:165
  144.5 2.7 scatter_custom_fusion.3
  160.1 3.1 gather_fusion.6
  166.9 3.4 fusion.112
  170.3 2.4 reduce_sum.241
  172.7 9.4 %all-to-all-start.3 = ((bf16[16,16,512]{2,1,0:T(8,128)(2,1)}), bf16[16,16,512]{2,1,0:T(8,128)(2,1)}, u32[]{:S(2)}, u32[]{:S(2)}) async-start(bf16[16,16,512]{2,1,0:T(8,128)(2,1)} %reduce_sum.241), calls=%async_computation.3 | async-start | bytes 524288 | tf_op jit(solution)/shard_map/all_to_all | solution.py:220
  182.2 7.7 %scatter_custom_fusion.6 = f32[128,512]{1,0:T(8,128)} fusion(s32[768]{0:T(1024)} %get-tuple-element.17, f32[]{:T(128)} %constant.20.clone.1, f32[768,512]{1,0:T(8,128)S(1)} %get-tuple-element.46), kind=kCustom, calls=%fused_computation.168 | custom fusion | flops 1179648 | bytes 1835520 | tf_op jit(solution)/shard_map/scatter-add | solution.py:214
  190.2 2.6 copy.33
  201.4 2.6 copy.32
  204.0 2.5 copy.38
  206.5 2.5 copy.39
  211.6 3.3 scatter_custom_fusion.5
  214.9 2.4 convolution_bitcast_fusion
  217.3 2.5 copy.31
  222.2 14.5 %pad_maximum_fusion = f32[4,787456]{1,0:T(4,128)} fusion(f32[1,787456]{1,0:T(1,128)} %bitcast.46, f32[1,787456]{1,0:T(1,128)S(1)} %bitcast.200, f32[1,787456]{1,0:T(1,128)} %bitcast.44, f32[1,787456]{1,0:T(1,128)S(1)} %bitcast.201), kind=kLoop, calls=%fused_computation.14 | loop fusion | flops 9449472 | bytes 25198592 | tf_op jit(solution)/shard_map/stack | solution.py:235
  241.1 2.2 fusion.43
  243.2 282.9 %all-reduce.3.cloned.1.call-done = f32[4,787456]{1,0:T(4,128)} async-done(((f32[4,787456]{1,0:T(4,128)}), f32[4,787456]{1,0:T(4,128)}) %all-reduce.3.cloned.1.call-update) | async-done | bytes 12599312
  (255 shorter events, 102.9 us)
Async XLA Ops:
  7.2 23.2 %copy-start.44 = (s32[1,16,16]{2,1,0:T(8,128)S(1)}, s32[1,16,16]{2,1,0:T(8,128)}, u32[]{:S(2)}) copy-start(s32[1,16,16]{2,1,0:T(8,128)} %param.23) | copy-start | bytes 3076
  7.2 22.5 %copy-start.43 = (s32[1,16,16]{2,1,0:T(8,128)S(1)}, s32[1,16,16]{2,1,0:T(8,128)}, u32[]{:S(2)}) copy-start(s32[1,16,16]{2,1,0:T(8,128)} %param.18) | copy-start | bytes 3076
  7.2 20.6 %copy-start.18 = (bf16[128,512]{1,0:T(8,128)(2,1)S(1)}, bf16[128,512]{1,0:T(8,128)(2,1)}, u32[]{:S(2)}) copy-start(bf16[128,512]{1,0:T(8,128)(2,1)} %param.13) | copy-start | bytes 393220
  10.7 25.0 %all-to-all-start = ((bf16[16,16,512]{2,1,0:T(8,128)(2,1)}), bf16[16,16,512]{2,1,0:T(8,128)(2,1)S(1)}, u32[]{:S(2)}, u32[]{:S(2)}) async-start(bf16[16,16,512]{2,1,0:T(8,128)(2,1)} %bitcast.2), calls=%async_computation | async-start | bytes 524288 | tf_op jit(solution)/shard_map/all_to_all | solution.py:91
  43.2 11.0 %copy-start.41 = (f32[1,512]{1,0:T(1,128)S(1)}, f32[1,512]{1,0:T(1,128)}, u32[]{:S(2)}) copy-start(f32[1,512]{1,0:T(1,128)} %get-tuple-element.28) | copy-start | bytes 6148
  53.5 10.9 %copy-start.58 = (f32[128]{0:T(128)}, f32[128]{0:T(128)S(1)}, u32[]{:S(2)}) copy-start(f32[128]{0:T(128)S(1)} %broadcast_multiply_fusion.11) | copy-start | bytes 1540
  53.7 10.8 %copy-start.60 = (f32[128]{0:T(128)}, f32[128]{0:T(128)S(1)}, u32[]{:S(2)}) copy-start(f32[128]{0:T(128)S(1)} %add_rsqrt_fusion.3) | copy-start | bytes 1540
  56.2 15.3 %all-to-all-start.1 = ((bf16[16,16,512]{2,1,0:T(8,128)(2,1)}), bf16[16,16,512]{2,1,0:T(8,128)(2,1)}, u32[]{:S(2)}, u32[]{:S(2)}) async-start(bf16[16,16,512]{2,1,0:T(8,128)(2,1)} %bitcast.19), calls=%async_computation.1 | async-start | bytes 524288 | tf_op jit(solution)/shard_map/all_to_all | solution.py:110
  64.5 8.5 %copy-start.51 = (s32[1024]{0:T(1024)S(1)}, s32[1024]{0:T(1024)}, u32[]{:S(2)}) copy-start(s32[1024]{0:T(1024)} %get-tuple-element.50) | copy-start | bytes 12292
  66.2 9.4 %copy-start.4 = (f32[512,512]{1,0:T(8,128)}, f32[512,512]{1,0:T(8,128)S(1)}, u32[]{:S(2)}) copy-start(f32[512,512]{1,0:T(8,128)S(1)} %gather_fusion.4) | copy-start | bytes 3145732
  80.7 10.2 %copy-start.36 = (bf16[128,512]{1,0:T(8,128)(2,1)S(1)}, bf16[128,512]{1,0:T(8,128)(2,1)}, u32[]{:S(2)}) copy-start(bf16[128,512]{1,0:T(8,128)(2,1)} %param.14) | copy-start | bytes 393220
  87.8 7.1 %copy-start.24 = (f32[128,512]{1,0:T(8,128)}, f32[128,512]{1,0:T(8,128)S(1)}, u32[]{:S(2)}) copy-start(f32[128,512]{1,0:T(8,128)S(1)} %scatter_custom_fusion.1) | copy-start | bytes 786436
  92.9 6.9 %copy-start.56 = (f32[1,512]{1,0:T(1,128)S(1)}, f32[1,512]{1,0:T(1,128)}, u32[]{:S(2)}) copy-start(f32[1,512]{1,0:T(1,128)} %get-tuple-element.27) | copy-start | bytes 6148
  103.6 6.4 %copy-start.55 = (f32[1,512]{1,0:T(1,128)S(1)}, f32[1,512]{1,0:T(1,128)}, u32[]{:S(2)}) copy-start(f32[1,512]{1,0:T(1,128)} %get-tuple-element.31) | copy-start | bytes 6148
  113.5 19.8 %copy-start.6 = (f32[64,4,8,128]{3,2,1,0:T(8,128)S(1)}, f32[64,4,8,128]{3,2,1,0:T(8,128)}, u32[]{:S(2)}) copy-start(f32[64,4,8,128]{3,2,1,0:T(8,128)} %convolution_bitcast_fusion.3) | copy-start | bytes 3145732
  126.3 18.1 %all-to-all-start.2 = ((bf16[16,16,512]{2,1,0:T(8,128)(2,1)}), bf16[16,16,512]{2,1,0:T(8,128)(2,1)}, u32[]{:S(2)}, u32[]{:S(2)}) async-start(bf16[16,16,512]{2,1,0:T(8,128)(2,1)} %bitcast.220), calls=%async_computation.2 | async-start | bytes 524288 | tf_op jit(solution)/shard_map/all_to_all | solution.py:165
  137.7 5.4 %copy-start.38 = (bf16[128,512]{1,0:T(8,128)(2,1)S(1)}, bf16[128,512]{1,0:T(8,128)(2,1)}, u32[]{:S(2)}) copy-start(bf16[128,512]{1,0:T(8,128)(2,1)} %param.14) | copy-start | bytes 393220
  138.0 6.5 %slice-start = ((f32[384,512]{1,0:T(8,128)}), f32[128,512]{1,0:T(8,128)S(1)}, s32[]{:S(2)}) async-start(f32[384,512]{1,0:T(8,128)} %scatter_custom_fusion.2), calls=%async_computation.5 | async-start | bytes 524288 | tf_op jit(solution)/shard_map/slice | solution.py:171
  139.3 10.6 %copy-start.17 = (f32[128,512]{1,0:T(8,128)S(1)}, f32[128,512]{1,0:T(8,128)}, u32[]{:S(2)}) copy-start(f32[128,512]{1,0:T(8,128)} %copy-done.16) | copy-start | bytes 786436
  139.3 10.6 %copy-start.42 = (f32[1,512]{1,0:T(1,128)S(1)}, f32[1,512]{1,0:T(1,128)}, u32[]{:S(2)}) copy-start(f32[1,512]{1,0:T(1,128)} %get-tuple-element.28) | copy-start | bytes 6148
  143.0 9.7 %copy-start.35 = (f32[128,512]{1,0:T(8,128)S(1)}, f32[128,512]{1,0:T(8,128)}, u32[]{:S(2)}) copy-start(f32[128,512]{1,0:T(8,128)} %copy-done.34) | copy-start | bytes 786436
  149.8 7.6 %copy-start.23 = (f32[128,512]{1,0:T(8,128)S(1)}, f32[128,512]{1,0:T(8,128)}, u32[]{:S(2)}) copy-start(f32[128,512]{1,0:T(8,128)} %copy-done.22) | copy-start | bytes 786436
  151.9 6.9 %copy-start.27 = (f32[128,512]{1,0:T(8,128)}, f32[128,512]{1,0:T(8,128)S(1)}, u32[]{:S(2)}) copy-start(f32[128,512]{1,0:T(8,128)S(1)} %get-tuple-element.44) | copy-start | bytes 786436
  152.7 7.4 %copy-start.40 = (s32[1024]{0:T(1024)S(1)}, s32[1024]{0:T(1024)}, u32[]{:S(2)}) copy-start(s32[1024]{0:T(1024)} %copy-done.39) | copy-start | bytes 12292
  154.7 5.4 %copy-start.30 = (bf16[128,512]{1,0:T(8,128)(2,1)}, bf16[128,512]{1,0:T(8,128)(2,1)S(1)}, u32[]{:S(2)}) copy-start(bf16[128,512]{1,0:T(8,128)(2,1)S(1)} %get-tuple-element.24) | copy-start | bytes 393220
  170.3 19.6 %copy-start.9 = (f32[64,4,8,128]{3,2,1,0:T(8,128)S(1)}, f32[64,4,8,128]{3,2,1,0:T(8,128)}, u32[]{:S(2)}) copy-start(f32[64,4,8,128]{3,2,1,0:T(8,128)} %convolution_bitcast_fusion.6) | copy-start | bytes 3145732
  172.7 38.9 %all-to-all-start.3 = ((bf16[16,16,512]{2,1,0:T(8,128)(2,1)}), bf16[16,16,512]{2,1,0:T(8,128)(2,1)}, u32[]{:S(2)}, u32[]{:S(2)}) async-start(bf16[16,16,512]{2,1,0:T(8,128)(2,1)} %reduce_sum.241), calls=%async_computation.3 | async-start | bytes 524288 | tf_op jit(solution)/shard_map/all_to_all | solution.py:220
  182.1 344.0 %all-reduce.3.cloned.1.call-start = ((), (), s32[]{:S(2)}) async-start(), calls=%async_computation.4 | async-start | bytes 25198592
  201.4 7.6 %copy-start.61 = (f32[512]{0:T(512)S(1)}, f32[512]{0:T(512)}, u32[]{:S(2)}) copy-start(f32[512]{0:T(512)} %get-tuple-element.47) | copy-start | bytes 6148
  201.4 7.6 %copy-start.59 = (f32[512]{0:T(512)S(1)}, f32[512]{0:T(512)}, u32[]{:S(2)}) copy-start(f32[512]{0:T(512)} %get-tuple-element.6) | copy-start | bytes 6148
  201.4 7.7 %copy-start.62 = (f32[512]{0:T(512)S(1)}, f32[512]{0:T(512)}, u32[]{:S(2)}) copy-start(f32[512]{0:T(512)} %get-tuple-element.23) | copy-start | bytes 6148
  201.4 8.9 %copy-start.52 = (f32[512]{0:T(512)S(1)}, f32[512]{0:T(512)}, u32[]{:S(2)}) copy-start(f32[512]{0:T(512)} %get-tuple-element.10) | copy-start | bytes 6148
  (38 other events, 103.7 us)
Sparse Core Ops, SparseCore 0:
  236.8 289.2 all-reduce.2
where the time goes:
time: 545 us; the launch traced here: 535 us
  waiting for transfers between devices  286 us (52%)
  other arithmetic  73.4 us (13%)
  local copies, waits for them, and re-layouts  65.9 us (12%)
  matrix products  59.9 us (11%)
  starting transfers between devices  34.6 us (6%)
  between operations  15.1 us (3%)
    unnamed x2, waiting for transfers between devices  283 us
    unnamed x156, local copies, waits for them, and re-layouts  25 us
    dot_general x12, matrix products, through_weight(): lax.dot_general(grad, weight, (((1,), (1,)), ((), ())), preferred_element...  23.9 us
    dot_general x12, matrix products, project(): return jnp.dot(left, weight, preferred_element_type=jnp.float32)  18.7 us
    dot_general x12, matrix products, row_contract(): lax.dot_general(left, right, (((0,), (0,)), ((), ())), preferred_element_...  17.4 us
    another operation x1, other arithmetic, local(): stacked = jnp.stack([grid_bucket, node_bucket, edge_bucket, top_bucket])  14.5 us
    all_to_all x1, starting transfers between devices, local(): lax.all_to_all(grid_latent[slot_rows], 'grid', split_axis=0, concat_axis=...  11.2 us
  transfers between devices with their start and end apart: 5, of which 2 were waited for; matrix products, arithmetic and copies ran while one was open for 12% of the time, Pallas kernels for 0%

commit v1 on v0

v1 whole, which is shorter than its diff:
```python
import functools
import math

import jax
import jax.numpy as jnp
import numpy as np
from jax import lax
from jax.experimental import pallas as pl
from jax.experimental.pallas import tpu as pltpu
from jax.sharding import PartitionSpec as P

bf16 = jnp.bfloat16
f32 = jnp.float32
epsilon = 1e-05
MESH = pl.DeviceIdType.MESH
PARTS = (2, 4, 2, 4, 4)


def mm(left, right):
    return jnp.dot(left, right, preferred_element_type=f32)


def tn(left, right):
    return lax.dot_general(left, right, (((0,), (0,)), ((), ())), preferred_element_type=f32)


def nt(left, right):
    return lax.dot_general(left, right, (((1,), (1,)), ((), ())), preferred_element_type=f32)


def row_mean(values):
    return jnp.mean(values, axis=-1, keepdims=True)


def column_sum(values):
    return jnp.sum(values, axis=0, keepdims=True)


def forward(x, out_weight):
    sigmoid = 0.5 * jnp.tanh(0.5 * x) + 0.5
    active = x * sigmoid
    slope = active * (1.0 - sigmoid) + sigmoid
    hidden = active.astype(bf16)
    projected = mm(hidden, out_weight)
    centered = projected - row_mean(projected)
    reciprocal = lax.rsqrt(row_mean(centered * centered) + epsilon)
    return hidden, slope, centered * reciprocal, reciprocal


def backward(upstream, gain, normed, reciprocal, slope, out_weight):
    gain_grad = column_sum(upstream * normed)
    weighted = upstream * gain
    inner = reciprocal * (weighted - row_mean(weighted) - normed * row_mean(weighted * normed))
    inner = inner.astype(bf16)
    summed_grad = nt(inner, out_weight) * slope
    return summed_grad.astype(bf16), inner, column_sum(summed_grad), gain_grad


def sizes(grid_dev, mesh_dev, features, edges, cap, fan):
    zh, ny, nc, zl, nx = PARTS
    own = 3 * features // (zh * ny * nc * zl * nx)
    pad = -(-own // 8) * 8
    return dict(
        G=grid_dev, M=mesh_dev, D=features, E=edges, cap=cap, fan=fan, zh=zh, ny=ny, nc=nc, zl=zl, nx=nx,
        nz=zh * zl, ng=zh * ny * nc, nm=zl * nx, own=own, pad=pad, out=-(-(own + 2) // 8) * 8,
        block=3 * features // (zh * ny * nc), plane=zh * zl * own,
    )


def constants(s):
    slots = s["ng"] * s["cap"]
    at = np.arange(slots)
    spread = (at[None, :] % s["cap"] == np.arange(s["cap"])[:, None]).astype(np.float32)
    mask = (at[None, :] // s["cap"] == np.arange(s["ng"])[:, None]).astype(np.float32)
    depth = (at % s["cap"]).astype(np.float32)[None, :]
    rows = s["nx"] * s["nz"] * s["own"]
    perm = np.zeros((rows, rows), np.float32)
    low = np.zeros((s["nz"] * 2 * s["pad"], s["plane"]), np.float32)
    high = np.zeros_like(low)
    for z in range(s["nz"]):
        for i in range(s["own"]):
            for x in range(s["nx"]):
                perm[x * s["plane"] + z * s["own"] + i, (z * s["nx"] + x) * s["own"] + i] = 1
            low[z * 2 * s["pad"] + i, z * s["own"] + i] = 1
            high[z * 2 * s["pad"] + s["pad"] + i, z * s["own"] + i] = 1
    return (
        jnp.asarray(spread, bf16), jnp.asarray(mask, f32), jnp.asarray(depth, f32),
        jnp.asarray(perm, bf16), jnp.asarray(low, bf16), jnp.asarray(high, bf16),
    )


def copies(s):
    kinds = dict(
        a2a=2 * (s["ng"] - 1) + 2 * (s["nm"] - 1), core=4, first=4 * (s["ny"] + s["nx"] - 2),
        second=4 * (s["ny"] + s["nx"] - 2), last=2 * (s["nz"] - 1),
        vec=1 + s["ny"] - 1 + s["nx"] - 1 + s["nz"] - 1, shift=1,
    )
    return sum(kinds.values())


def kernel(
    s, scale,
    grid_latent, mesh_latent, cotangent, weights, biases, gains, send_rows, counts, targets, senders, receivers,
    halo_rows, spread, mask, depth, perm, low_pad, high_pad,
    mesh_out, grid_grad, mesh_grad, shares,
    w, send_hot, target_hot, halo_hot, edge_hot,
    slot_out, slot_in, halo_out, halo_in, back_out, back_in, slot_back_out, slot_back_in,
    slot_terms, hidden0, slope0, normed0, recip0, inner0, slot_sum, gather_sum, receiver_sum,
    table, hidden2, slope2, normed2, recip2, inner2, grad2,
    bucket, core_in, split, first_in, partial, second_in, plane, last_out, last_in,
    vec, vec_sum, vec_in, shift_out, shift_in,
    weight_sem, send_sem, recv_sem,
):
    D, M, cap, fan = s["D"], s["M"], s["cap"], s["fan"]
    zh, ny, nc, zl, nx, nz, ng, nm = (s[k] for k in ("zh", "ny", "nc", "zl", "nx", "nz", "ng", "nm"))
    gi, mi = lax.axis_index("grid"), lax.axis_index("mesh")
    core = gi % nc
    y = (gi // nc) % ny
    z_hi = gi // (nc * ny)
    x = mi % nx
    z_lo = mi // nx
    z = z_hi * zl + z_lo
    flat = gi * nm + mi
    total = ng * nm

    def at_core(o):
        return ((z_hi * ny + y) * nc + (core + o) % nc, mi)

    def at_y(o):
        return ((z_hi * ny + (y + o) % ny) * nc + core, mi)

    def at_x(o):
        return (gi, z_lo * nx + (x + o) % nx)

    def at_z(o):
        to = (z + o) % nz
        return (((to // zl) * ny + y) * nc + core, (to % zl) * nx + x)

    def at_flat(o):
        to = (flat + o + total) % total
        return (to // nm, to % nm)

    order = (1, 3, 0, 2, 4, 5, 6, 7, 9, 8, 10, 11)
    loads = {i: pltpu.make_async_copy(weights.at[i], w.at[i], weight_sem.at[i]) for i in order}
    for i in order:
        loads[i].start()

    barrier = pltpu.get_barrier_semaphore()
    greeted = [((gi + o) % ng, mi) for o in range(1, ng)] + [(gi, (mi + o) % nm) for o in range(1, nm)]
    for a in range(1, zh):
        for b in range(1, zl):
            greeted.append(
                ((((z_hi + a) % zh) * ny + y) * nc + core, ((z_lo + b) % zl) * nx + x)
            )
    greeted += [at_flat(1), at_flat(-1)]
    for device in greeted:
        pl.semaphore_signal(barrier, inc=1, device_id=device, device_id_type=MESH)

    ids = iter(range(copies(s)))
    started = []

    def send(source, target, device):
        i = next(ids)
        copy = pltpu.make_async_remote_copy(
            src_ref=source, dst_ref=target, send_sem=send_sem.at[i], recv_sem=recv_sem.at[i],
            device_id=device, device_id_type=MESH,
        )
        copy.start()
        started.append(copy)
        return copy

    def arrive(batch):
        for copy in batch:
            copy.wait_recv()

    def exchange_grid(out, into):
        batch = [send(out.at[(gi + o) % ng], into.at[gi], ((gi + o) % ng, mi)) for o in range(1, ng)]
        into[pl.ds(gi, 1)] = out[pl.ds(gi, 1)]
        return batch

    def exchange_mesh(out, into):
        batch = [send(out.at[(mi + o) % nm], into.at[mi], (gi, (mi + o) % nm)) for o in range(1, nm)]
        into[pl.ds(mi, 1)] = out[pl.ds(mi, 1)]
        return batch

    def lay(values):
        spread_out = mm(values.astype(f32).astype(bf16), spread[...])
        return column_sum(spread_out * mask[...])

    def one_hot(rows, nodes):
        node = lax.broadcasted_iota(jnp.int32, (nodes, rows.shape[1]), 0).astype(f32)
        return jnp.where(node == rows, 1.0, 0.0).astype(bf16)

    send_hot[...] = one_hot(lay(send_rows[0]), s["G"])
    slot_out[...] = tn(send_hot[...], grid_latent[...]).astype(bf16).reshape(slot_out.shape)
    pl.semaphore_wait(barrier, len(greeted))
    slots_batch = exchange_grid(slot_out, slot_in)

    count_row = mm(counts[...].astype(f32).astype(bf16), mask[...].astype(bf16))
    live = depth[...] < count_row
    for k in range(fan):
        target_hot[k] = one_hot(jnp.where(live, lay(targets[0, k]), -1.0), M)
    halo_hot[...] = one_hot(lay(halo_rows[0]), M)
    tiles, _, tile = edge_hot.shape
    joined = M + nm * cap
    for t in range(tiles):
        part = pl.ds(t * tile, tile)
        edge_hot[t, :joined] = one_hot(senders[:, part].astype(f32), joined)
        edge_hot[t, joined:] = one_hot(receivers[:, part].astype(f32), M)

    loads[1].wait()
    latent = mesh_latent[...]
    receiver_terms = mm(latent, w[1]).astype(bf16)
    loads[3].wait()
    low_part = mm(latent, w[3])
    loads[0].wait()
    loads[2].wait()

    arrive(slots_batch)
    slot_terms[...] = mm(slot_in[...].reshape(ng * cap, D), w[0]).astype(bf16)
    gather_sum[...] = jnp.zeros_like(gather_sum)

    def encode(k, carry):
        hot = target_hot[k]
        x0 = slot_terms[...].astype(f32) + tn(hot, receiver_terms) + biases[0:1, :]
        hidden, slope, normed, recip = forward(x0, w[2])
        hidden0[k] = hidden
        slope0[k] = slope
        normed0[k] = normed
        recip0[k] = recip
        gather_sum[...] += mm(hot, (normed * gains[0:1, :]).astype(bf16))
        return carry

    lax.fori_loop(0, fan, encode, 0)
    grid_gathered = gather_sum[...].astype(bf16)

    loads[4].wait()
    loads[5].wait()
    x1 = low_part + mm(grid_gathered, w[4]) + biases[1:2, :]
    hidden1, slope1, normed1, recip1 = forward(x1, w[5])
    middle = (latent.astype(f32) + normed1 * gains[1:2, :]).astype(bf16)
    halo_out[...] = tn(halo_hot[...], middle).astype(bf16).reshape(halo_out.shape)
    halo_batch = exchange_mesh(halo_out, halo_in)

    for i in (6, 7, 9, 8):
        loads[i].wait()
    table[:M] = mm(middle, w[6]).astype(bf16)
    table[joined:] = mm(middle, w[7]).astype(bf16)
    top_part = mm(middle, w[9]) + biases[3:4, :]

    arrive(halo_batch)
    halo_rows_in = halo_in[...].reshape(nm * cap, D)
    table[M:joined] = mm(halo_rows_in, w[6]).astype(bf16)
    gather_sum[...] = jnp.zeros_like(gather_sum)

    def process(t, carry):
        x2 = tn(edge_hot[t], table[...]) + biases[2:3, :]
        hidden, slope, normed, recip = forward(x2, w[8])
        hidden2[t] = hidden
        slope2[t] = slope
        normed2[t] = normed
        recip2[t] = recip
        gather_sum[...] += mm(edge_hot[t, joined:], (normed * gains[2:3, :]).astype(bf16))
        return carry

    lax.fori_loop(0, tiles, process, 0)
    mesh_gathered = gather_sum[...].astype(bf16)

    loads[10].wait()
    loads[11].wait()
    x3 = top_part + mm(mesh_gathered, w[10])
    hidden3, slope3, normed3, recip3 = forward(x3, w[11])
    mesh_out[...] = (middle.astype(f32) + normed3 * gains[3:4, :]).astype(bf16)
    upstream = cotangent[...].astype(f32)
    grad3, inner3, bias_grad, gain_grad = backward(upstream, gains[3:4, :], normed3, recip3, slope3, w[11])
    vec[6:7, :] = bias_grad
    vec[7:8, :] = gain_grad
    gathered_grad = nt(grad3, w[10]).astype(bf16)
    middle_part = upstream + nt(grad3, w[9])

    def put(j, m, value):
        value = value.astype(bf16)
        for r in range(0, D, 32):
            a, rest = divmod(m * D + r, ny * nc * s["block"])
            b, rest = divmod(rest, nc * s["block"])
            c, q = divmod(rest, s["block"])
            bucket[j, c, b, a * s["block"] + q : a * s["block"] + q + 32, :] = value[r : r + 32]

    half = D // 2
    rows = s["plane"]
    waiting = {}

    def core_start(j):
        waiting["core", j] = [send(bucket.at[j, 1 - core], core_in.at[j], at_core(1))]

    def first_start(j):
        arrive(waiting["core", j])

        def fold(b, carry):
            both = bucket[j, core, b].astype(f32) + core_in[j, b].astype(f32)
            moved = mm(perm[...], both.astype(bf16)).astype(bf16)
            for a in range(nx):
                split[j, 0, b, a] = moved[a * rows : (a + 1) * rows, :half]
                split[j, 1, a, b] = moved[a * rows : (a + 1) * rows, half:]
            return carry

        lax.fori_loop(0, ny, fold, 0)
        waiting["first", j] = [
            send(split.at[j, 0, (y + o) % ny], first_in.at[j, 0, o - 1], at_y(o)) for o in range(1, ny)
        ] + [send(split.at[j, 1, (x + o) % nx], first_in.at[j, 1, o - 1], at_x(o)) for o in range(1, nx)]

    def second_start(j):
        arrive(waiting["first", j])
        for h, mine, n in ((0, y, ny), (1, x, nx)):
            value = split[j, h, mine].astype(f32)
            for o in range(n - 1):
                value = value + first_in[j, h, o].astype(f32)
            partial[j, h] = value.astype(bf16)
        waiting["second", j] = [
            send(partial.at[j, 0, (x + o) % nx], second_in.at[j, 0, o - 1], at_x(o)) for o in range(1, nx)
        ] + [send(partial.at[j, 1, (y + o) % ny], second_in.at[j, 1, o - 1], at_y(o)) for o in range(1, ny)]

    def second_finish(j):
        arrive(waiting["second", j])
        for h, mine, n in ((0, x, nx), (1, y, ny)):
            value = partial[j, h, mine].astype(f32)
            for o in range(n - 1):
                value = value + second_in[j, h, o].astype(f32)
            plane[j, :, h * half : (h + 1) * half] = value.astype(bf16)

    def last_start(p):
        padded = mm(low_pad[...], plane[2 * p]) + mm(high_pad[...], plane[2 * p + 1])
        last_out[p] = padded.astype(bf16).reshape(last_out.shape[1:])
        waiting["last", p] = [
            send(last_out.at[p, (z + o) % nz], last_in.at[p, o - 1], at_z(o)) for o in range(1, nz)
        ]

    def last_finish(p):
        arrive(waiting["last", p])
        value = last_out[p, z].astype(f32)
        for o in range(nz - 1):
            value = value + last_in[p, o].astype(f32)
        return value * scale

    put(3, 0, tn(middle, grad3))
    put(3, 1, tn(mesh_gathered, grad3))
    put(3, 2, tn(hidden3, inner3))
    core_start(3)

    vec[4:6, :] = jnp.zeros((2, D), f32)

    def process_back(t, carry):
        up = tn(edge_hot[t, joined:], gathered_grad)
        grad, inner, bias_part, gain_part = backward(up, gains[2:3, :], normed2[t], recip2[t], slope2[t], w[8])
        inner2[t] = inner
        grad2[t] = grad
        vec[4:5, :] += bias_part
        vec[5:6, :] += gain_part
        return carry

    lax.fori_loop(0, tiles, process_back, 0)
    spread_grad = mm(edge_hot[0], grad2[0])
    for t in range(1, tiles):
        spread_grad = spread_grad + mm(edge_hot[t], grad2[t])
    spread_half = spread_grad.astype(bf16)
    back_out[...] = spread_half[M:joined].reshape(back_out.shape)
    back_batch = exchange_mesh(back_out, back_in)
    receiver_half = spread_half[joined:]
    first_start(3)
    put(2, 0, tn(middle, spread_half[:M]) + tn(halo_rows_in, spread_half[M:joined]))
    put(2, 1, tn(middle, receiver_half))
    put(2, 2, tn(hidden2[...].reshape(tiles * tile, D), inner2[...].reshape(tiles * tile, D)))
    core_start(2)
    middle_part = middle_part + nt(receiver_half, w[7])
    arrive(back_batch)
    returned = mm(halo_hot[...], back_in[...].reshape(nm * cap, D))
    sender_half = (spread_grad[:M] + returned).astype(bf16)
    middle_grad = middle_part + nt(sender_half, w[6])

    grad1, inner1, bias_grad, gain_grad = backward(middle_grad, gains[1:2, :], normed1, recip1, slope1, w[5])
    vec[2:3, :] = bias_grad
    vec[3:4, :] = gain_grad
    low_gathered_grad = nt(grad1, w[4]).astype(bf16)
    lower_part = middle_grad + nt(grad1, w[3])
    put(1, 0, tn(latent, grad1))
    put(1, 1, tn(grid_gathered, grad1))
    put(1, 2, tn(hidden1, inner1))
    core_start(1)
    first_start(2)
    second_start(3)

    vec[0:2, :] = jnp.zeros((2, D), f32)
    slot_sum[...] = jnp.zeros_like(slot_sum)
    receiver_sum[...] = jnp.zeros_like(receiver_sum)

    def encode_back(k, carry):
        hot = target_hot[k]
        up = tn(hot, low_gathered_grad)
        grad, inner, bias_part, gain_part = backward(up, gains[0:1, :], normed0[k], recip0[k], slope0[k], w[2])
        inner0[k] = inner
        slot_sum[...] += grad.astype(f32)
        receiver_sum[...] += mm(hot, grad)
        vec[0:1, :] += bias_part
        vec[1:2, :] += gain_part
        return carry

    lax.fori_loop(0, fan, encode_back, 0)
    slot_half = slot_sum[...].astype(bf16)
    slot_back_out[...] = slot_half.reshape(slot_back_out.shape)
    slot_back_batch = exchange_grid(slot_back_out, slot_back_in)
    waiting["vec", 0] = [send(vec, vec_in.at[0], at_core(1))]
    receiver_low = receiver_sum[...].astype(bf16)
    put(0, 0, tn(slot_in[...].reshape(ng * cap, D), slot_half))
    put(0, 1, tn(latent, receiver_low))
    put(0, 2, tn(hidden0[...].reshape(fan * ng * cap, D), inner0[...].reshape(fan * ng * cap, D)))
    core_start(0)
    first_start(1)
    second_start(2)
    second_finish(3)
    mesh_grad[...] = lower_part + nt(receiver_low, w[1])
    first_start(0)

    at = 0

    def vec_step(batch_key, level, steps, start):
        arrive(waiting[batch_key])
        value = vec[...] if level == 0 else vec_sum[level - 1]
        for o in steps:
            value = value + vec_in[o]
        return value

    vec_sum[0] = vec_step(("vec", 0), 0, range(0, 1), 0)
    waiting["vec", 1] = [send(vec_sum.at[0], vec_in.at[o], at_y(o)) for o in range(1, ny)]
    second_finish(2)
    last_start(1)
    second_start(1)
    vec_sum[1] = vec_step(("vec", 1), 1, range(1, ny), 0)
    waiting["vec", 2] = [send(vec_sum.at[1], vec_in.at[ny - 1 + o], at_x(o)) for o in range(1, nx)]

    arrive(slot_back_batch)
    grid_half = mm(send_hot[...], slot_back_in[...].reshape(ng * cap, D)).astype(bf16)
    grid_grad[...] = nt(grid_half, w[0])

    second_start(0)
    vec_sum[2] = vec_step(("vec", 2), 2, range(ny, ny + nx - 1), 0)
    base = ny + nx - 2
    waiting["vec", 3] = [send(vec_sum.at[2], vec_in.at[base + o], at_z(o)) for o in range(1, nz)]
    second_finish(1)
    second_finish(0)
    last_start(0)
    upper = last_finish(1)
    vec_total = vec_step(("vec", 3), 3, range(base + 1, base + nz), 0) * scale
    lower = last_finish(0)
    pad = s["pad"]
    results = (lower[:pad], lower[pad:], upper[:pad], upper[pad:])
    first_device = flat == 0
    for j in range(4):
        shift_out[2 * j : 2 * j + 2, :] = jnp.where(first_device, vec_total[2 * j : 2 * j + 2], results[j][:2])
    shift = send(shift_out, shift_in, at_flat(-1))
    own = s["own"]
    for j in range(4):
        shares[j, :own, :] = results[j][:own]
    arrive([shift])
    for j in range(4):
        shares[j, own : own + 2, :] = shift_in[2 * j : 2 * j + 2, :]
    for copy in started:
        copy.wait_send()


def local(grid_latent, mesh_latent, mesh_cotangent, weights, biases, norm_gains, send_rows, counts, targets,
          senders, receivers, halo_rows):
    G, D = grid_latent.shape
    M = mesh_latent.shape[0]
    fan, sources, cap = targets.shape[1:]
    E = senders.shape[1]
    s = sizes(G, M, D, E, cap, fan)
    ng, nm, ny, nx, nz = s["ng"], s["nm"], s["ny"], s["nx"], s["nz"]
    slots = ng * cap
    tiles = 2
    tile = E // tiles
    joined = M + nm * cap
    half = D // 2
    n = copies(s)
    scale = 1.0 / math.sqrt(M * ng * nm)
    vmem = pl.BlockSpec(memory_space=pltpu.VMEM)
    scratch = [
        pltpu.VMEM(weights.shape, bf16),
        pltpu.VMEM((G, slots), bf16), pltpu.VMEM((fan, M, slots), bf16), pltpu.VMEM((M, nm * cap), bf16),
        pltpu.VMEM((tiles, joined + M, tile), bf16),
        pltpu.VMEM((ng, cap, D), bf16), pltpu.VMEM((ng, cap, D), bf16),
        pltpu.VMEM((nm, cap, D), bf16), pltpu.VMEM((nm, cap, D), bf16),
        pltpu.VMEM((nm, cap, D), bf16), pltpu.VMEM((nm, cap, D), bf16),
        pltpu.VMEM((ng, cap, D), bf16), pltpu.VMEM((ng, cap, D), bf16),
        pltpu.VMEM((slots, D), bf16),
        pltpu.VMEM((fan, slots, D), bf16), pltpu.VMEM((fan, slots, D), f32), pltpu.VMEM((fan, slots, D), f32),
        pltpu.VMEM((fan, slots, 1), f32), pltpu.VMEM((fan, slots, D), bf16),
        pltpu.VMEM((slots, D), f32), pltpu.VMEM((M, D), f32), pltpu.VMEM((M, D), f32),
        pltpu.VMEM((joined + M, D), bf16),
        pltpu.VMEM((tiles, tile, D), bf16), pltpu.VMEM((tiles, tile, D), f32), pltpu.VMEM((tiles, tile, D), f32),
        pltpu.VMEM((tiles, tile, 1), f32), pltpu.VMEM((tiles, tile, D), bf16), pltpu.VMEM((tiles, tile, D), bf16),
        pltpu.VMEM((4, 2, ny, s["zh"] * s["block"], D), bf16),
        pltpu.VMEM((4, ny, s["zh"] * s["block"], D), bf16),
        pltpu.VMEM((4, 2, nx, nx, s["plane"], half), bf16),
        pltpu.VMEM((4, 2, nx - 1, nx, s["plane"], half), bf16),
        pltpu.VMEM((4, 2, nx, s["plane"], half), bf16),
        pltpu.VMEM((4, 2, nx - 1, s["plane"], half), bf16),
        pltpu.VMEM((4, s["plane"], D), bf16),
        pltpu.VMEM((2, nz, 2 * s["pad"], D), bf16),
        pltpu.VMEM((2, nz - 1, 2 * s["pad"], D), bf16),
        pltpu.VMEM((8, D), f32), pltpu.VMEM((3, 8, D), f32), pltpu.VMEM((ny + nx + nz - 2, 8, D), f32),
        pltpu.VMEM((8, D), f32), pltpu.VMEM((8, D), f32),
        pltpu.SemaphoreType.DMA((weights.shape[0],)),
        pltpu.SemaphoreType.DMA((n,)), pltpu.SemaphoreType.DMA((n,)),
    ]
    mesh_out, grid_grad, mesh_grad, shares = pl.pallas_call(
        functools.partial(kernel, s, scale),
        out_shape=(
            jax.ShapeDtypeStruct((M, D), bf16), jax.ShapeDtypeStruct((G, D), f32),
            jax.ShapeDtypeStruct((M, D), f32), jax.ShapeDtypeStruct((4, s["out"], D), f32),
        ),
        in_specs=[vmem] * 3 + [pl.BlockSpec(memory_space=pl.ANY)] + [vmem] * 14,
        out_specs=(vmem,) * 4,
        scratch_shapes=scratch,
        compiler_params=pltpu.CompilerParams(
            collective_id=0, has_side_effects=True, vmem_limit_bytes=60 * 1024 * 1024
        ),
    )(
        grid_latent, mesh_latent, mesh_cotangent, weights, biases, norm_gains, send_rows, counts, targets,
        senders, receivers, halo_rows, *constants(s),
    )
    extra = 2 * D // (ng * nm)
    start = (lax.axis_index("grid") * nm + lax.axis_index("mesh")) * extra
    weight_grad = lax.dynamic_slice(
        shares.reshape(4, s["out"] * D), (0, start), (4, s["own"] * D + extra)
    )
    return mesh_out, grid_grad, mesh_grad, weight_grad


def solution(mesh):
    both = ("grid", "mesh")
    placed = (
        P(both, None), P(both, None), P(both, None), P(), P(), P(), P(both, None, None), P(both, None),
        P(both, None, None, None), P(both, None), P(both, None), P(both, None, None),
    )
    return jax.shard_map(
        local, mesh=mesh, in_specs=placed,
        out_specs=(P(both, None), P(both, None), P(both, None), P(None, both)),
        check_vma=False,
    )
```

time: 545 us -> 96.4 us (0.18); the launches traced: 535 us -> 96.2 us
  waiting for transfers between devices: 286 us -> 0 us
  Pallas kernels: 0 us -> 88.8 us
  other arithmetic: 73.4 us -> 0 us
  matrix products: 59.9 us -> 0 us
  local copies, waits for them, and re-layouts: 65.9 us -> 6.71 us
  starting transfers between devices: 34.6 us -> 0 us
  between operations: 15.1 us -> 0.65 us
    unnamed x2 -> x0, waiting for transfers between devices: 283 us -> none
    pallas_call x0 -> x1, Pallas kernels: none -> 88.8 us  [local(): pl.pallas_call(functools.partial(kernel, s, scale), out_shape=(jax.ShapeD...]
    dot_general x36 -> x0, matrix products: 59.9 us -> none  [the longest x12 23.9 us: through_weight(): lax.dot_general(grad, weight, (((1,), (1,)), ((), ())), preferred_element...]
    scatter-add x7 -> x0, other arithmetic: 35.1 us -> none  [the longest x1 7.67 us: local(): jax.ops.segment_sum(grid_float, target_index, num_segments=node_count)]
    all_to_all x4 -> x0, starting transfers between devices: 34.6 us -> none  [the longest x1 11.2 us: local(): lax.all_to_all(grid_latent[slot_rows], 'grid', split_axis=0, concat_axis=...]
    gather x9 -> x0, local copies, waits for them, and re-layouts: 20.3 us -> none  [the longest x2 5 us: local(): mesh_gathered_grad[receivers]]
    unnamed x156 -> x4, local copies, waits for them, and re-layouts: 25 us -> 5.99 us
    another operation x1 -> x0, other arithmetic: 14.5 us -> none  [local(): stacked = jnp.stack([grid_bucket, node_bucket, edge_bucket, top_bucket])]
  transfers between devices with their start and end apart: 5 -> 0, of which waited for: 2 -> 0; matrix products, arithmetic and copies ran while one was open for 12% -> 0% of each run, Pallas kernels for 0% -> 0%
where the time goes in v1:
time: 96.4 us; the launch traced here: 96.2 us
  Pallas kernels  88.8 us (92%)
  local copies, waits for them, and re-layouts  6.71 us (7%)
    pallas_call x1, Pallas kernels, local(): pl.pallas_call(functools.partial(kernel, s, scale), out_shape=(jax.ShapeD...  88.8 us
    unnamed x4, local copies, waits for them, and re-layouts  5.99 us

profile of v1, /device:TPU:6, one launch (start us, length us, event | category | flops | bytes accessed | tf_op | source)
XLA Modules:
  0.0 96.2 jit_solution(11967149461870103486)
XLA Ops:
  0.6 88.8 %shard_map.201 = (bf16[128,512]{1,0:T(8,128)(2,1)}, f32[256,512]{1,0:T(8,128)}, f32[128,512]{1,0:T(8,128)}, f32[4,8,512]{2,1,0:T(8,128)}) custom-call(bf16[256,512]{1,0:T(8,128)(2,1)} %grid_latent.1, bf16[128,512]{1,0:T(8,128)(2,1)} %mesh_latent.1, bf16[128,512]{1,0:T(8,128)(2,1)} %cotangent.1, bf16[12,512,512]{2,1,0:T(8,128)(2,1)} %weights.1, ...), custom_call_target="tpu_custom_call" | custom-call | tf_op jit(solution)/shard_map/pallas_call | solution.py:515
  89.5 0.9 copy.22
  90.3 0.7 constant_dynamic-slice_fusion
  91.1 1.6 %copy.26 = bf16[128,512]{1,0:T(8,128)(2,1)} copy(bf16[128,512]{1,0:T(8,128)(2,1)} %get-tuple-element.16) | data formatting | bytes 262144
  92.6 1.9 %copy.27 = f32[256,512]{1,0:T(8,128)} copy(f32[256,512]{1,0:T(8,128)} %get-tuple-element.17) | data formatting | bytes 1048576
  94.5 1.7 %copy.28 = f32[128,512]{1,0:T(8,128)} copy(f32[128,512]{1,0:T(8,128)} %get-tuple-element.18) | data formatting | bytes 524288

commit v2 on v1

--- a/solution.py
+++ b/solution.py
@@ -84,8 +84,8 @@
             low[z * 2 * s["pad"] + i, z * s["own"] + i] = 1
             high[z * 2 * s["pad"] + s["pad"] + i, z * s["own"] + i] = 1
     return (
-        jnp.asarray(spread, bf16), jnp.asarray(mask, f32), jnp.asarray(depth, f32),
-        jnp.asarray(perm, bf16), jnp.asarray(low, bf16), jnp.asarray(high, bf16),
+        jnp.asarray(spread, f32), jnp.asarray(mask, f32), jnp.asarray(depth, f32),
+        jnp.asarray(perm, f32), jnp.asarray(low, f32), jnp.asarray(high, f32),
     )
 
 
@@ -100,7 +100,8 @@
 
 def kernel(
     s, scale,
-    grid_latent, mesh_latent, cotangent, weights, biases, gains, send_rows, counts, targets, senders, receivers,
+    sources, weights, mesh_out_hbm, grid_grad_hbm, mesh_grad_hbm, shares_hbm,
+    grid_latent, mesh_latent, cotangent, biases, gains, send_rows, counts, targets, senders, receivers,
     halo_rows, spread, mask, depth, perm, low_pad, high_pad,
     mesh_out, grid_grad, mesh_grad, shares,
     w, send_hot, target_hot, halo_hot, edge_hot,
@@ -109,7 +110,7 @@
     table, hidden2, slope2, normed2, recip2, inner2, grad2,
     bucket, core_in, split, first_in, partial, second_in, plane, last_out, last_in,
     vec, vec_sum, vec_in, shift_out, shift_in,
-    weight_sem, send_sem, recv_sem,
+    weight_sem, input_sem, output_sem, send_sem, recv_sem,
 ):
     D, M, cap, fan = s["D"], s["M"], s["cap"], s["fan"]
     zh, ny, nc, zl, nx, nz, ng, nm = (s[k] for k in ("zh", "ny", "nc", "zl", "nx", "nz", "ng", "nm"))
@@ -140,6 +141,20 @@
         to = (flat + o + total) % total
         return (to // nm, to % nm)
 
+    operands = (
+        send_rows, spread, mask, grid_latent, counts, depth, targets, halo_rows, senders, receivers,
+        mesh_latent, biases, gains, cotangent, perm, low_pad, high_pad,
+    )
+    fetch = [pltpu.make_async_copy(a, b, input_sem.at[i]) for i, (a, b) in enumerate(zip(sources, operands))]
+    for copy in fetch:
+        copy.start()
+    results_out = []
+
+    def store(value_ref, target):
+        copy = pltpu.make_async_copy(value_ref, target, output_sem.at[len(results_out)])
+        copy.start()
+        results_out.append(copy)
+
     order = (1, 3, 0, 2, 4, 5, 6, 7, 9, 8, 10, 11)
     loads = {i: pltpu.make_async_copy(weights.at[i], w.at[i], weight_sem.at[i]) for i in order}
     for i in order:
@@ -184,18 +199,22 @@
         return batch
 
     def lay(values):
-        spread_out = mm(values.astype(f32).astype(bf16), spread[...])
+        spread_out = mm(values.astype(f32).astype(bf16), spread[...].astype(bf16))
         return column_sum(spread_out * mask[...])
 
     def one_hot(rows, nodes):
         node = lax.broadcasted_iota(jnp.int32, (nodes, rows.shape[1]), 0).astype(f32)
         return jnp.where(node == rows, 1.0, 0.0).astype(bf16)
 
+    for copy in fetch[:4]:
+        copy.wait()
     send_hot[...] = one_hot(lay(send_rows[0]), s["G"])
     slot_out[...] = tn(send_hot[...], grid_latent[...]).astype(bf16).reshape(slot_out.shape)
     pl.semaphore_wait(barrier, len(greeted))
     slots_batch = exchange_grid(slot_out, slot_in)
 
+    for copy in fetch[4:]:
+        copy.wait()
     count_row = mm(counts[...].astype(f32).astype(bf16), mask[...].astype(bf16))
     live = depth[...] < count_row
     for k in range(fan):
@@ -271,6 +290,7 @@
     x3 = top_part + mm(mesh_gathered, w[10])
     hidden3, slope3, normed3, recip3 = forward(x3, w[11])
     mesh_out[...] = (middle.astype(f32) + normed3 * gains[3:4, :]).astype(bf16)
+    store(mesh_out, mesh_out_hbm)
     upstream = cotangent[...].astype(f32)
     grad3, inner3, bias_grad, gain_grad = backward(upstream, gains[3:4, :], normed3, recip3, slope3, w[11])
     vec[6:7, :] = bias_grad
@@ -298,7 +318,7 @@
 
         def fold(b, carry):
             both = bucket[j, core, b].astype(f32) + core_in[j, b].astype(f32)
-            moved = mm(perm[...], both.astype(bf16)).astype(bf16)
+            moved = mm(perm[...].astype(bf16), both.astype(bf16)).astype(bf16)
             for a in range(nx):
                 split[j, 0, b, a] = moved[a * rows : (a + 1) * rows, :half]
                 split[j, 1, a, b] = moved[a * rows : (a + 1) * rows, half:]
@@ -329,7 +349,7 @@
             plane[j, :, h * half : (h + 1) * half] = value.astype(bf16)
 
     def last_start(p):
-        padded = mm(low_pad[...], plane[2 * p]) + mm(high_pad[...], plane[2 * p + 1])
+        padded = mm(low_pad[...].astype(bf16), plane[2 * p]) + mm(high_pad[...].astype(bf16), plane[2 * p + 1])
         last_out[p] = padded.astype(bf16).reshape(last_out.shape[1:])
         waiting["last", p] = [
             send(last_out.at[p, (z + o) % nz], last_in.at[p, o - 1], at_z(o)) for o in range(1, nz)
@@ -418,9 +438,8 @@
     second_start(2)
     second_finish(3)
     mesh_grad[...] = lower_part + nt(receiver_low, w[1])
+    store(mesh_grad, mesh_grad_hbm)
     first_start(0)
-
-    at = 0
 
     def vec_step(batch_key, level, steps, start):
         arrive(waiting[batch_key])
@@ -440,6 +459,7 @@
     arrive(slot_back_batch)
     grid_half = mm(send_hot[...], slot_back_in[...].reshape(ng * cap, D)).astype(bf16)
     grid_grad[...] = nt(grid_half, w[0])
+    store(grid_grad, grid_grad_hbm)
 
     second_start(0)
     vec_sum[2] = vec_step(("vec", 2), 2, range(ny, ny + nx - 1), 0)
@@ -459,12 +479,48 @@
     shift = send(shift_out, shift_in, at_flat(-1))
     own = s["own"]
     for j in range(4):
-        shares[j, :own, :] = results[j][:own]
+        for r in range(own):
+            shares[r, j : j + 1, :] = results[j][r : r + 1]
     arrive([shift])
     for j in range(4):
-        shares[j, own : own + 2, :] = shift_in[2 * j : 2 * j + 2, :]
+        for r in range(2):
+            shares[own + r, j : j + 1, :] = shift_in[2 * j + r : 2 * j + r + 1, :]
+    store(shares, shares_hbm)
     for copy in started:
         copy.wait_send()
+    for copy in results_out:
+        copy.wait()
+
+
+def whole(s, scale, count, *refs):
+    kernel(s, scale, refs[:count], *refs[count:])
+
+
+def finish(s, total, upper, grid, lower, shares, upper_out, grid_out, lower_out, weight_out, *scratch):
+    held, sem = scratch[:3], scratch[3]
+    n = len(held)
+    fetch = [
+        pltpu.make_async_copy(source, target, sem.at[i])
+        for i, (source, target) in enumerate(zip((upper, grid, lower), held))
+    ]
+    drain = [
+        pltpu.make_async_copy(source, target, sem.at[n + i])
+        for i, (source, target) in enumerate(zip(held, (upper_out, grid_out, lower_out)))
+    ]
+    for copy in fetch:
+        copy.start()
+    for here, there in zip(fetch, drain):
+        here.wait()
+        there.start()
+    D = s["D"]
+    joined = jnp.concatenate([shares[r] for r in range(s["out"])], axis=1)
+    width = s["out"] * D
+    extra = 2 * D // total
+    start = (lax.axis_index("grid") * s["nm"] + lax.axis_index("mesh")) * extra
+    rolled = pltpu.roll(joined, (width - start) % width, 1)
+    weight_out[...] = rolled[:4, : s["own"] * D + extra]
+    for copy in drain:
+        copy.wait()
 
 
 def local(grid_latent, mesh_latent, mesh_cotangent, weights, biases, norm_gains, send_rows, counts, targets,
@@ -483,7 +539,20 @@
     n = copies(s)
     scale = 1.0 / math.sqrt(M * ng * nm)
     vmem = pl.BlockSpec(memory_space=pltpu.VMEM)
-    scratch = [
+    spread, mask, depth, perm, low_pad, high_pad = constants(s)
+    operands = (
+        send_rows, spread, mask, grid_latent, counts, depth, targets, halo_rows, senders, receivers,
+        mesh_latent, biases, norm_gains, mesh_cotangent, perm, low_pad, high_pad,
+    )
+    named = (
+        grid_latent, mesh_latent, mesh_cotangent, biases, norm_gains, send_rows, counts, targets, senders, receivers,
+        halo_rows, spread, mask, depth, perm, low_pad, high_pad,
+    )
+    results = (
+        jax.ShapeDtypeStruct((M, D), bf16), jax.ShapeDtypeStruct((G, D), f32),
+        jax.ShapeDtypeStruct((M, D), f32), jax.ShapeDtypeStruct((s["out"], 8, D), f32),
+    )
+    scratch = [pltpu.VMEM(v.shape, v.dtype) for v in named + results] + [
         pltpu.VMEM(weights.shape, bf16),
         pltpu.VMEM((G, slots), bf16), pltpu.VMEM((fan, M, slots), bf16), pltpu.VMEM((M, nm * cap), bf16),
         pltpu.VMEM((tiles, joined + M, tile), bf16),
@@ -510,30 +579,34 @@
         pltpu.VMEM((8, D), f32), pltpu.VMEM((3, 8, D), f32), pltpu.VMEM((ny + nx + nz - 2, 8, D), f32),
         pltpu.VMEM((8, D), f32), pltpu.VMEM((8, D), f32),
         pltpu.SemaphoreType.DMA((weights.shape[0],)),
+        pltpu.SemaphoreType.DMA((len(operands),)), pltpu.SemaphoreType.DMA((4,)),
         pltpu.SemaphoreType.DMA((n,)), pltpu.SemaphoreType.DMA((n,)),
     ]
+    anywhere = pl.BlockSpec(memory_space=pl.ANY)
     mesh_out, grid_grad, mesh_grad, shares = pl.pallas_call(
-        functools.partial(kernel, s, scale),
-        out_shape=(
-            jax.ShapeDtypeStruct((M, D), bf16), jax.ShapeDtypeStruct((G, D), f32),
-            jax.ShapeDtypeStruct((M, D), f32), jax.ShapeDtypeStruct((4, s["out"], D), f32),
-        ),
-        in_specs=[vmem] * 3 + [pl.BlockSpec(memory_space=pl.ANY)] + [vmem] * 14,
-        out_specs=(vmem,) * 4,
+        functools.partial(whole, s, scale, len(operands)),
+        out_shape=results,
+        in_specs=[anywhere] * (len(operands) + 1),
+        out_specs=(anywhere,) * 4,
         scratch_shapes=scratch,
         compiler_params=pltpu.CompilerParams(
             collective_id=0, has_side_effects=True, vmem_limit_bytes=60 * 1024 * 1024
         ),
-    )(
-        grid_latent, mesh_latent, mesh_cotangent, weights, biases, norm_gains, send_rows, counts, targets,
-        senders, receivers, halo_rows, *constants(s),
-    )
-    extra = 2 * D // (ng * nm)
-    start = (lax.axis_index("grid") * nm + lax.axis_index("mesh")) * extra
-    weight_grad = lax.dynamic_slice(
-        shares.reshape(4, s["out"] * D), (0, start), (4, s["own"] * D + extra)
-    )
-    return mesh_out, grid_grad, mesh_grad, weight_grad
+    )(*operands, weights)
+    return tuple(
+        pl.pallas_call(
+            functools.partial(finish, s, ng * nm),
+            out_shape=(
+                jax.ShapeDtypeStruct((M, D), bf16), jax.ShapeDtypeStruct((G, D), f32),
+                jax.ShapeDtypeStruct((M, D), f32),
+                jax.ShapeDtypeStruct((4, s["own"] * D + 2 * D // (ng * nm)), f32),
+            ),
+            in_specs=[anywhere] * 3 + [vmem],
+            out_specs=(anywhere, anywhere, anywhere, vmem),
+            scratch_shapes=[pltpu.VMEM(v.shape, v.dtype) for v in results[:3]] + [pltpu.SemaphoreType.DMA((6,))],
+            compiler_params=pltpu.CompilerParams(vmem_limit_bytes=60 * 1024 * 1024),
+        )(mesh_out, grid_grad, mesh_grad, shares)
+    )
 
 
 def solution(mesh):

time: 96.4 us -> 91.6 us (0.950)
  local copies, waits for them, and re-layouts: 6.71 us -> 0 us
  Pallas kernels: 88.8 us -> 90.8 us
    unnamed x4 -> x0, local copies, waits for them, and re-layouts: 5.99 us -> none
    pallas_call x1 -> x2, Pallas kernels: 88.8 us -> 90.8 us  [the longest x1 87.3 us: local(): pl.pallas_call(functools.partial(whole, s, scale, len(operands)), out_sha...]
where the time goes in v2:
time: 91.6 us; the launch traced here: 91.5 us
  Pallas kernels  90.8 us (99%)
    pallas_call x1, Pallas kernels, local(): pl.pallas_call(functools.partial(whole, s, scale, len(operands)), out_sha...  87.3 us
    pallas_call x1, Pallas kernels, local(): pl.pallas_call(functools.partial(finish, s, ng * nm), out_shape=(jax.Shap...  3.57 us

profile of v2, /device:TPU:6, one launch (start us, length us, event | category | flops | bytes accessed | tf_op | source)
XLA Modules:
  0.0 91.5 jit_solution(11860671236721310318)
XLA Ops:
  0.6 87.3 %shard_map.201 = (bf16[128,512]{1,0:T(8,128)(2,1)}, f32[256,512]{1,0:T(8,128)}, f32[128,512]{1,0:T(8,128)}, f32[8,8,512]{2,1,0:T(8,128)}) custom-call(s32[1,16,16]{2,1,0:T(8,128)} %refs_0_.1, f32[16,256]{1,0:T(8,128)} %constant.12.clone.refs_1_, f32[16,256]{1,0:T(8,128)} %constant.13.clone.refs_2_, bf16[256,512]{1,0:T(8,128)(2,1)} %refs_3_.1, ...), custom_call_target="tpu_custom_call" | custom-call | tf_op jit(solution)/shard_map/pallas_call | solution.py:586
  87.9 3.6 %shard_map.202 = (bf16[128,512]{1,0:T(8,128)(2,1)}, f32[256,512]{1,0:T(8,128)}, f32[128,512]{1,0:T(8,128)}, f32[4,3076]{1,0:T(4,128)}) custom-call(bf16[128,512]{1,0:T(8,128)(2,1)} %get-tuple-element.8.upper, f32[256,512]{1,0:T(8,128)} %get-tuple-element.9.grid, f32[128,512]{1,0:T(8,128)} %get-tuple-element.10.lower, f32[8,8,512]{2,1,0:T(8,128)} %get-tuple-element.11.shares), custom_call_target="tpu_custom_call" | custom-call | tf_op jit(solution)/shard_map/pallas_call | solution.py:597

commit v3 on v2

--- a/solution.py
+++ b/solution.py
@@ -106,7 +106,7 @@
     mesh_out, grid_grad, mesh_grad, shares,
     w, send_hot, target_hot, halo_hot, edge_hot,
     slot_out, slot_in, halo_out, halo_in, back_out, back_in, slot_back_out, slot_back_in,
-    slot_terms, hidden0, slope0, normed0, recip0, inner0, slot_sum, gather_sum, receiver_sum,
+    hidden0, slope0, normed0, recip0, inner0, gather_sum,
     table, hidden2, slope2, normed2, recip2, inner2, grad2,
     bucket, core_in, split, first_in, partial, second_in, plane, last_out, last_in,
     vec, vec_sum, vec_in, shift_out, shift_in,
@@ -146,7 +146,7 @@
         mesh_latent, biases, gains, cotangent, perm, low_pad, high_pad,
     )
     fetch = [pltpu.make_async_copy(a, b, input_sem.at[i]) for i, (a, b) in enumerate(zip(sources, operands))]
-    for copy in fetch:
+    for copy in fetch[:4]:
         copy.start()
     results_out = []
 
@@ -157,8 +157,6 @@
 
     order = (1, 3, 0, 2, 4, 5, 6, 7, 9, 8, 10, 11)
     loads = {i: pltpu.make_async_copy(weights.at[i], w.at[i], weight_sem.at[i]) for i in order}
-    for i in order:
-        loads[i].start()
 
     barrier = pltpu.get_barrier_semaphore()
     greeted = [((gi + o) % ng, mi) for o in range(1, ng)] + [(gi, (mi + o) % nm) for o in range(1, nm)]
@@ -184,17 +182,31 @@
         started.append(copy)
         return copy
 
+    def far_first(n):
+        return sorted(range(1, n), key=lambda o: -min(o, n - o))
+
     def arrive(batch):
         for copy in batch:
             copy.wait_recv()
 
-    def exchange_grid(out, into):
-        batch = [send(out.at[(gi + o) % ng], into.at[gi], ((gi + o) % ng, mi)) for o in range(1, ng)]
-        into[pl.ds(gi, 1)] = out[pl.ds(gi, 1)]
+    ring = ny * nc
+    lane = gi % ring
+
+    def exchange_grid(out, into, dz):
+        batch = []
+        for o in range(1 if dz == 0 else 0, ring):
+            to = ((z_hi + dz) % zh) * ring + (lane + o) % ring
+            batch.append(send(out.at[to], into.at[gi], (to, mi)))
+        if dz == 0:
+            into[pl.ds(gi, 1)] = out[pl.ds(gi, 1)]
         return batch
 
     def exchange_mesh(out, into):
-        batch = [send(out.at[(mi + o) % nm], into.at[mi], (gi, (mi + o) % nm)) for o in range(1, nm)]
+        batch = []
+        for dz in sorted(range(zl), key=lambda d: -min(d, zl - d)):
+            for o in range(1 if dz == 0 else 0, nx):
+                to = ((z_lo + dz) % zl) * nx + (x + o) % nx
+                batch.append(send(out.at[to], into.at[mi], (gi, to)))
         into[pl.ds(mi, 1)] = out[pl.ds(mi, 1)]
         return batch
 
@@ -211,21 +223,34 @@
     send_hot[...] = one_hot(lay(send_rows[0]), s["G"])
     slot_out[...] = tn(send_hot[...], grid_latent[...]).astype(bf16).reshape(slot_out.shape)
     pl.semaphore_wait(barrier, len(greeted))
-    slots_batch = exchange_grid(slot_out, slot_in)
-
+    slots_batch = [None] * zh
+    for dz in reversed(range(zh)):
+        slots_batch[dz] = exchange_grid(slot_out, slot_in, dz)
+
+    for copy in fetch[4:11]:
+        copy.start()
+    for i in order[:4]:
+        loads[i].start()
+    for copy in fetch[11:]:
+        copy.start()
+    for i in order[4:]:
+        loads[i].start()
     for copy in fetch[4:]:
         copy.wait()
     count_row = mm(counts[...].astype(f32).astype(bf16), mask[...].astype(bf16))
     live = depth[...] < count_row
+    part = ring * cap
     for k in range(fan):
-        target_hot[k] = one_hot(jnp.where(live, lay(targets[0, k]), -1.0), M)
+        target_row = jnp.where(live, lay(targets[0, k]), -1.0)
+        for a in range(zh):
+            target_hot[a, :, k * part : (k + 1) * part] = one_hot(target_row[:, a * part : (a + 1) * part], M)
     halo_hot[...] = one_hot(lay(halo_rows[0]), M)
     tiles, _, tile = edge_hot.shape
     joined = M + nm * cap
     for t in range(tiles):
-        part = pl.ds(t * tile, tile)
-        edge_hot[t, :joined] = one_hot(senders[:, part].astype(f32), joined)
-        edge_hot[t, joined:] = one_hot(receivers[:, part].astype(f32), M)
+        piece = pl.ds(t * tile, tile)
+        edge_hot[t, :joined] = one_hot(senders[:, piece].astype(f32), joined)
+        edge_hot[t, joined:] = one_hot(receivers[:, piece].astype(f32), M)
 
     loads[1].wait()
     latent = mesh_latent[...]
@@ -235,23 +260,22 @@
     loads[0].wait()
     loads[2].wait()
 
-    arrive(slots_batch)
-    slot_terms[...] = mm(slot_in[...].reshape(ng * cap, D), w[0]).astype(bf16)
-    gather_sum[...] = jnp.zeros_like(gather_sum)
-
-    def encode(k, carry):
-        hot = target_hot[k]
-        x0 = slot_terms[...].astype(f32) + tn(hot, receiver_terms) + biases[0:1, :]
+    gathered = None
+    for t in range(zh):
+        away = (z_hi + t) % zh
+        arrive(slots_batch[t])
+        here = pl.ds(away * ring, ring)
+        terms = mm(slot_in[here].reshape(part, D), w[0]).astype(bf16).astype(f32)
+        hot = target_hot[away]
+        x0 = jnp.concatenate([terms] * fan, axis=0) + tn(hot, receiver_terms) + biases[0:1, :]
         hidden, slope, normed, recip = forward(x0, w[2])
-        hidden0[k] = hidden
-        slope0[k] = slope
-        normed0[k] = normed
-        recip0[k] = recip
-        gather_sum[...] += mm(hot, (normed * gains[0:1, :]).astype(bf16))
-        return carry
-
-    lax.fori_loop(0, fan, encode, 0)
-    grid_gathered = gather_sum[...].astype(bf16)
+        hidden0[t] = hidden
+        slope0[t] = slope
+        normed0[t] = normed
+        recip0[t] = recip
+        message = mm(hot, (normed * gains[0:1, :]).astype(bf16))
+        gathered = message if gathered is None else gathered + message
+    grid_gathered = gathered.astype(bf16)
 
     loads[4].wait()
     loads[5].wait()
@@ -326,8 +350,13 @@
 
         lax.fori_loop(0, ny, fold, 0)
         waiting["first", j] = [
-            send(split.at[j, 0, (y + o) % ny], first_in.at[j, 0, o - 1], at_y(o)) for o in range(1, ny)
-        ] + [send(split.at[j, 1, (x + o) % nx], first_in.at[j, 1, o - 1], at_x(o)) for o in range(1, nx)]
+            send(split.at[j, 0, (y + o) % ny], first_in.at[j, 0, o - 1], at_y(o)) for o in far_first(ny)
+        ]
+
+    def first_other(j):
+        waiting["first", j] += [
+            send(split.at[j, 1, (x + o) % nx], first_in.at[j, 1, o - 1], at_x(o)) for o in far_first(nx)
+        ]
 
     def second_start(j):
         arrive(waiting["first", j])
@@ -337,8 +366,8 @@
                 value = value + first_in[j, h, o].astype(f32)
             partial[j, h] = value.astype(bf16)
         waiting["second", j] = [
-            send(partial.at[j, 0, (x + o) % nx], second_in.at[j, 0, o - 1], at_x(o)) for o in range(1, nx)
-        ] + [send(partial.at[j, 1, (y + o) % ny], second_in.at[j, 1, o - 1], at_y(o)) for o in range(1, ny)]
+            send(partial.at[j, 0, (x + o) % nx], second_in.at[j, 0, o - 1], at_x(o)) for o in far_first(nx)
+        ] + [send(partial.at[j, 1, (y + o) % ny], second_in.at[j, 1, o - 1], at_y(o)) for o in far_first(ny)]
 
     def second_finish(j):
         arrive(waiting["second", j])
@@ -352,7 +381,7 @@
         padded = mm(low_pad[...].astype(bf16), plane[2 * p]) + mm(high_pad[...].astype(bf16), plane[2 * p + 1])
         last_out[p] = padded.astype(bf16).reshape(last_out.shape[1:])
         waiting["last", p] = [
-            send(last_out.at[p, (z + o) % nz], last_in.at[p, o - 1], at_z(o)) for o in range(1, nz)
+            send(last_out.at[p, (z + o) % nz], last_in.at[p, o - 1], at_z(o)) for o in far_first(nz)
         ]
 
     def last_finish(p):
@@ -392,7 +421,10 @@
     put(2, 2, tn(hidden2[...].reshape(tiles * tile, D), inner2[...].reshape(tiles * tile, D)))
     core_start(2)
     middle_part = middle_part + nt(receiver_half, w[7])
+    first_start(2)
     arrive(back_batch)
+    first_other(3)
+    first_other(2)
     returned = mm(halo_hot[...], back_in[...].reshape(nm * cap, D))
     sender_half = (spread_grad[:M] + returned).astype(bf16)
     middle_grad = middle_part + nt(sender_half, w[6])
@@ -401,59 +433,59 @@
     vec[2:3, :] = bias_grad
     vec[3:4, :] = gain_grad
     low_gathered_grad = nt(grad1, w[4]).astype(bf16)
-    lower_part = middle_grad + nt(grad1, w[3])
-    put(1, 0, tn(latent, grad1))
-    put(1, 1, tn(grid_gathered, grad1))
-    put(1, 2, tn(hidden1, inner1))
-    core_start(1)
-    first_start(2)
-    second_start(3)
-
-    vec[0:2, :] = jnp.zeros((2, D), f32)
-    slot_sum[...] = jnp.zeros_like(slot_sum)
-    receiver_sum[...] = jnp.zeros_like(receiver_sum)
-
-    def encode_back(k, carry):
-        hot = target_hot[k]
+
+    slot_back_batch = []
+    receiver_low = None
+    totals = []
+    for t in reversed(range(zh)):
+        away = (z_hi + t) % zh
+        hot = target_hot[away]
         up = tn(hot, low_gathered_grad)
-        grad, inner, bias_part, gain_part = backward(up, gains[0:1, :], normed0[k], recip0[k], slope0[k], w[2])
-        inner0[k] = inner
-        slot_sum[...] += grad.astype(f32)
-        receiver_sum[...] += mm(hot, grad)
-        vec[0:1, :] += bias_part
-        vec[1:2, :] += gain_part
-        return carry
-
-    lax.fori_loop(0, fan, encode_back, 0)
-    slot_half = slot_sum[...].astype(bf16)
-    slot_back_out[...] = slot_half.reshape(slot_back_out.shape)
-    slot_back_batch = exchange_grid(slot_back_out, slot_back_in)
+        grad, inner, bias_part, gain_part = backward(up, gains[0:1, :], normed0[t], recip0[t], slope0[t], w[2])
+        inner0[t] = inner
+        slot_grad = grad[:part].astype(f32)
+        for k in range(1, fan):
+            slot_grad = slot_grad + grad[k * part : (k + 1) * part].astype(f32)
+        slot_back_out[pl.ds(away * ring, ring)] = slot_grad.astype(bf16).reshape(ring, cap, D)
+        slot_back_batch += exchange_grid(slot_back_out, slot_back_in, t)
+        low = mm(hot, grad)
+        receiver_low = low if receiver_low is None else receiver_low + low
+        totals.append((bias_part, gain_part))
+        if t == zh - 1:
+            put(1, 0, tn(latent, grad1))
+            put(1, 1, tn(grid_gathered, grad1))
+            put(1, 2, tn(hidden1, inner1))
+            core_start(1)
+    vec[0:1, :] = sum(a for a, _ in totals[1:]) + totals[0][0]
+    vec[1:2, :] = sum(b for _, b in totals[1:]) + totals[0][1]
     waiting["vec", 0] = [send(vec, vec_in.at[0], at_core(1))]
-    receiver_low = receiver_sum[...].astype(bf16)
-    put(0, 0, tn(slot_in[...].reshape(ng * cap, D), slot_half))
+    receiver_low = receiver_low.astype(bf16)
+    put(0, 2, tn(hidden0[...].reshape(fan * ng * cap, D), inner0[...].reshape(fan * ng * cap, D)))
+    put(0, 0, tn(slot_in[...].reshape(ng * cap, D), slot_back_out[...].reshape(ng * cap, D)))
     put(0, 1, tn(latent, receiver_low))
-    put(0, 2, tn(hidden0[...].reshape(fan * ng * cap, D), inner0[...].reshape(fan * ng * cap, D)))
     core_start(0)
     first_start(1)
-    second_start(2)
-    second_finish(3)
-    mesh_grad[...] = lower_part + nt(receiver_low, w[1])
-    store(mesh_grad, mesh_grad_hbm)
+    first_other(1)
     first_start(0)
-
-    def vec_step(batch_key, level, steps, start):
-        arrive(waiting[batch_key])
+    first_other(0)
+
+    def vec_step(level, steps):
+        arrive(waiting["vec", level])
         value = vec[...] if level == 0 else vec_sum[level - 1]
         for o in steps:
             value = value + vec_in[o]
         return value
 
-    vec_sum[0] = vec_step(("vec", 0), 0, range(0, 1), 0)
+    second_start(3)
+    second_start(2)
+    vec_sum[0] = vec_step(0, range(0, 1))
     waiting["vec", 1] = [send(vec_sum.at[0], vec_in.at[o], at_y(o)) for o in range(1, ny)]
+    mesh_grad[...] = middle_grad + nt(grad1, w[3]) + nt(receiver_low, w[1])
+    store(mesh_grad, mesh_grad_hbm)
+    second_finish(3)
     second_finish(2)
     last_start(1)
-    second_start(1)
-    vec_sum[1] = vec_step(("vec", 1), 1, range(1, ny), 0)
+    vec_sum[1] = vec_step(1, range(1, ny))
     waiting["vec", 2] = [send(vec_sum.at[1], vec_in.at[ny - 1 + o], at_x(o)) for o in range(1, nx)]
 
     arrive(slot_back_batch)
@@ -461,15 +493,19 @@
     grid_grad[...] = nt(grid_half, w[0])
     store(grid_grad, grid_grad_hbm)
 
-    second_start(0)
-    vec_sum[2] = vec_step(("vec", 2), 2, range(ny, ny + nx - 1), 0)
+    second_start(1)
+    vec_sum[2] = vec_step(2, range(ny, ny + nx - 1))
     base = ny + nx - 2
     waiting["vec", 3] = [send(vec_sum.at[2], vec_in.at[base + o], at_z(o)) for o in range(1, nz)]
+    second_start(0)
     second_finish(1)
     second_finish(0)
+    sent = len(started)
     last_start(0)
     upper = last_finish(1)
-    vec_total = vec_step(("vec", 3), 3, range(base + 1, base + nz), 0) * scale
+    for copy in started[:sent]:
+        copy.wait_send()
+    vec_total = vec_step(3, range(base + 1, base + nz)) * scale
     lower = last_finish(0)
     pad = s["pad"]
     results = (lower[:pad], lower[pad:], upper[:pad], upper[pad:])
@@ -486,7 +522,7 @@
         for r in range(2):
             shares[own + r, j : j + 1, :] = shift_in[2 * j + r : 2 * j + r + 1, :]
     store(shares, shares_hbm)
-    for copy in started:
+    for copy in started[sent:]:
         copy.wait_send()
     for copy in results_out:
         copy.wait()
@@ -496,29 +532,25 @@
     kernel(s, scale, refs[:count], *refs[count:])
 
 
-def finish(s, total, upper, grid, lower, shares, upper_out, grid_out, lower_out, weight_out, *scratch):
-    held, sem = scratch[:3], scratch[3]
-    n = len(held)
-    fetch = [
-        pltpu.make_async_copy(source, target, sem.at[i])
-        for i, (source, target) in enumerate(zip((upper, grid, lower), held))
-    ]
-    drain = [
-        pltpu.make_async_copy(source, target, sem.at[n + i])
-        for i, (source, target) in enumerate(zip(held, (upper_out, grid_out, lower_out)))
-    ]
-    for copy in fetch:
-        copy.start()
-    for here, there in zip(fetch, drain):
-        here.wait()
-        there.start()
+def finish(s, total, *refs):
+    sources, targets, held, turned, sem = refs[:4], refs[4:8], refs[8:12], refs[12], refs[13]
+    fetch = [pltpu.make_async_copy(a, b, sem.at[i]) for i, (a, b) in enumerate(zip(sources, held))]
+    ready = tuple(held[:3]) + (turned,)
+    drain = [pltpu.make_async_copy(a, b, sem.at[4 + i]) for i, (a, b) in enumerate(zip(ready, targets))]
+    for i in (3, 1, 2, 0):
+        fetch[i].start()
+    fetch[3].wait()
     D = s["D"]
-    joined = jnp.concatenate([shares[r] for r in range(s["out"])], axis=1)
+    joined = jnp.concatenate([held[3][r] for r in range(s["out"])], axis=1)
     width = s["out"] * D
     extra = 2 * D // total
     start = (lax.axis_index("grid") * s["nm"] + lax.axis_index("mesh")) * extra
     rolled = pltpu.roll(joined, (width - start) % width, 1)
-    weight_out[...] = rolled[:4, : s["own"] * D + extra]
+    for i in (1, 2, 0):
+        fetch[i].wait()
+        drain[i].start()
+    turned[...] = rolled[:4, : s["own"] * D + extra]
+    drain[3].start()
     for copy in drain:
         copy.wait()
 
@@ -532,6 +564,7 @@
     s = sizes(G, M, D, E, cap, fan)
     ng, nm, ny, nx, nz = s["ng"], s["nm"], s["ny"], s["nx"], s["nz"]
     slots = ng * cap
+    wide = fan * slots // s["zh"]
     tiles = 2
     tile = E // tiles
     joined = M + nm * cap
@@ -554,16 +587,15 @@
     )
     scratch = [pltpu.VMEM(v.shape, v.dtype) for v in named + results] + [
         pltpu.VMEM(weights.shape, bf16),
-        pltpu.VMEM((G, slots), bf16), pltpu.VMEM((fan, M, slots), bf16), pltpu.VMEM((M, nm * cap), bf16),
+        pltpu.VMEM((G, slots), bf16), pltpu.VMEM((s["zh"], M, wide), bf16), pltpu.VMEM((M, nm * cap), bf16),
         pltpu.VMEM((tiles, joined + M, tile), bf16),
         pltpu.VMEM((ng, cap, D), bf16), pltpu.VMEM((ng, cap, D), bf16),
         pltpu.VMEM((nm, cap, D), bf16), pltpu.VMEM((nm, cap, D), bf16),
         pltpu.VMEM((nm, cap, D), bf16), pltpu.VMEM((nm, cap, D), bf16),
         pltpu.VMEM((ng, cap, D), bf16), pltpu.VMEM((ng, cap, D), bf16),
-        pltpu.VMEM((slots, D), bf16),
-        pltpu.VMEM((fan, slots, D), bf16), pltpu.VMEM((fan, slots, D), f32), pltpu.VMEM((fan, slots, D), f32),
-        pltpu.VMEM((fan, slots, 1), f32), pltpu.VMEM((fan, slots, D), bf16),
-        pltpu.VMEM((slots, D), f32), pltpu.VMEM((M, D), f32), pltpu.VMEM((M, D), f32),
+        pltpu.VMEM((s["zh"], wide, D), bf16), pltpu.VMEM((s["zh"], wide, D), f32),
+        pltpu.VMEM((s["zh"], wide, D), f32), pltpu.VMEM((s["zh"], wide, 1), f32),
+        pltpu.VMEM((s["zh"], wide, D), bf16), pltpu.VMEM((M, D), f32),
         pltpu.VMEM((joined + M, D), bf16),
         pltpu.VMEM((tiles, tile, D), bf16), pltpu.VMEM((tiles, tile, D), f32), pltpu.VMEM((tiles, tile, D), f32),
         pltpu.VMEM((tiles, tile, 1), f32), pltpu.VMEM((tiles, tile, D), bf16), pltpu.VMEM((tiles, tile, D), bf16),
@@ -601,9 +633,10 @@
                 jax.ShapeDtypeStruct((M, D), f32),
                 jax.ShapeDtypeStruct((4, s["own"] * D + 2 * D // (ng * nm)), f32),
             ),
-            in_specs=[anywhere] * 3 + [vmem],
-            out_specs=(anywhere, anywhere, anywhere, vmem),
-            scratch_shapes=[pltpu.VMEM(v.shape, v.dtype) for v in results[:3]] + [pltpu.SemaphoreType.DMA((6,))],
+            in_specs=[anywhere] * 4,
+            out_specs=(anywhere,) * 4,
+            scratch_shapes=[pltpu.VMEM(v.shape, v.dtype) for v in results]
+            + [pltpu.VMEM((4, s["own"] * D + 2 * D // (ng * nm)), f32), pltpu.SemaphoreType.DMA((8,))],
             compiler_params=pltpu.CompilerParams(vmem_limit_bytes=60 * 1024 * 1024),
         )(mesh_out, grid_grad, mesh_grad, shares)
     )

time: 91.6 us -> 88.5 us (0.966)
  Pallas kernels: 90.8 us -> 87.6 us
    pallas_call x1, Pallas kernels: 87.3 us -> 85.5 us  [local(): pl.pallas_call(functools.partial(whole, s, scale, len(operands)), out_sha...]
    pallas_call x1, Pallas kernels: 3.57 us -> 2.11 us  [local(): pl.pallas_call(functools.partial(finish, s, ng * nm), out_shape=(jax.Shap...]
where the time goes in v3:
time: 88.5 us; the launch traced here: 88.4 us
  Pallas kernels  87.6 us (99%)
    pallas_call x1, Pallas kernels, local(): pl.pallas_call(functools.partial(whole, s, scale, len(operands)), out_sha...  85.5 us
    pallas_call x1, Pallas kernels, local(): pl.pallas_call(functools.partial(finish, s, ng * nm), out_shape=(jax.Shap...  2.11 us

profile of v3, /device:TPU:6, one launch (start us, length us, event | category | flops | bytes accessed | tf_op | source)
XLA Modules:
  0.0 88.4 jit_solution(15213835448156627031)
XLA Ops:
  0.6 85.5 %shard_map.201 = (bf16[128,512]{1,0:T(8,128)(2,1)}, f32[256,512]{1,0:T(8,128)}, f32[128,512]{1,0:T(8,128)}, f32[8,8,512]{2,1,0:T(8,128)}) custom-call(s32[1,16,16]{2,1,0:T(8,128)} %refs_0_.1, f32[16,256]{1,0:T(8,128)} %constant.12.clone.refs_1_, f32[16,256]{1,0:T(8,128)} %constant.13.clone.refs_2_, bf16[256,512]{1,0:T(8,128)(2,1)} %refs_3_.1, ...), custom_call_target="tpu_custom_call" | custom-call | tf_op jit(solution)/shard_map/pallas_call | solution.py:618
  86.1 2.1 %shard_map.202 = (bf16[128,512]{1,0:T(8,128)(2,1)}, f32[256,512]{1,0:T(8,128)}, f32[128,512]{1,0:T(8,128)}, f32[4,3076]{1,0:T(4,128)}) custom-call(bf16[128,512]{1,0:T(8,128)(2,1)} %get-tuple-element.8.refs_0_, f32[256,512]{1,0:T(8,128)} %get-tuple-element.9.refs_1_, f32[128,512]{1,0:T(8,128)} %get-tuple-element.10.refs_2_, ...), custom_call_target="tpu_custom_call" | custom-call | tf_op jit(solution)/shard_map/pallas_call | solution.py:629
